TPU v7x, 512 devices: a whole 4x4x16 slice. The times are simulated.
512 devices in a mesh: row: 32 (over x, y, core), col: 16 (over z).
Axes of the slice: x: 4, y: 4, z: 16, core: 2. Of those that a mesh axis runs over, the one named last changes fastest.
Arguments:
- diag_factor: float32 [1024, 1024], P('row', 'col'), may hold values from -1 to 2.5, as said below
- panel_factor: float32 [16384, 1024], P('row', 'col'), may hold values from -0.046875 to 0.046875
- left_factor: float32 [16384, 8192], P('row', 'col'), may hold values from -0.046875 to 0.046875
- pivot_factor: float32 [1024, 8192], P('row', 'col'), may hold values from -0.1875 to 0.1875
- panel_adjoint: float32 [16384, 1024], P('row', 'col'), may hold values from -6 to 6
- left_adjoint: float32 [16384, 8192], P('row', 'col'), may hold values from -6 to 6
- pivot_adjoint: float32 [1024, 8192], P('row', 'col'), may hold values from -6 to 6
- diag_adjoint: float32 [1024, 1024], P('row', 'col'), may hold values from -6 to 6
Outputs:
- solved_panel: float32 [16384, 1024], P('row', 'col')
- left_out: float32 [16384, 8192], P('row', 'col')
- pivot_out: float32 [1024, 8192], P('row', 'col')
- diag_out: float32 [1024, 1024], P('row', 'col')
Inputs may be any that keep to these rules, and one draw needn't show every extreme that they name: diag_factor is lower triangular: zero above the diagonal, diagonal entries at least 1.
All inputs are finite; a program needn't handle non-finite values.
Results may differ from a plain program's by a relative error of at most 0.000073.
Values sent between devices are 32-bit elements; how exact they have to be, the bound alone decides.
A program may use at most 64 MiB of HBM per device.

v0:
```python
import jax
import jax.numpy as jnp
from jax import lax
from jax.sharding import PartitionSpec as P


def right_solve(tile, source):
    return jax.scipy.linalg.solve_triangular(tile, source.T, trans="T", lower=True).T


def local(
    diag_factor,
    panel_factor,
    left_factor,
    pivot_factor,
    panel_adjoint,
    left_adjoint,
    pivot_adjoint,
    diag_adjoint,
):
    highest = lax.Precision.HIGHEST
    block_width = panel_adjoint.shape[1]
    my_col = lax.axis_index("col")
    my_row = lax.axis_index("row")
    column_block = lax.all_gather(diag_factor, "row", axis=0, tiled=True)
    whole_diag = lax.all_gather(column_block, "col", axis=1, tiled=True)
    full_rows = lax.all_gather(panel_adjoint, "col", axis=1, tiled=True)
    solved = right_solve(whole_diag, full_rows)
    solved_panel = lax.dynamic_slice_in_dim(solved, my_col * block_width, block_width, 1)
    picked = solved
    left_out = left_adjoint - jnp.dot(
        picked,
        lax.all_gather(pivot_factor, "row", axis=0, tiled=True),
        precision=highest,
        preferred_element_type=jnp.float32,
    )
    own_rows = diag_adjoint.shape[0]
    picked = solved
    pivot_sum = lax.psum_scatter(
        jnp.einsum("rk,rc->kc", picked, left_factor, precision=highest),
        "row",
        scatter_dimension=0,
        tiled=True,
    )
    picked = solved
    square_sum = lax.psum_scatter(
        jnp.einsum("rk,rc->kc", picked, panel_factor, precision=highest),
        "row",
        scatter_dimension=0,
        tiled=True,
    )
    pivot_out = pivot_adjoint - pivot_sum
    global_row = my_row * own_rows + lax.broadcasted_iota(jnp.int32, (own_rows, block_width), 0)
    global_col = my_col * block_width + lax.broadcasted_iota(jnp.int32, (own_rows, block_width), 1)
    diag_out = diag_adjoint - jnp.where(global_col <= global_row, square_sum, 0.0)
    return (solved_panel, left_out, pivot_out, diag_out)


def solution(mesh):
    in_specs = (
        P("row", "col"),
        P("row", "col"),
        P("row", "col"),
        P("row", "col"),
        P("row", "col"),
        P("row", "col"),
        P("row", "col"),
        P("row", "col"),
    )
    out_specs = (P("row", "col"), P("row", "col"), P("row", "col"), P("row", "col"))
    return jax.shard_map(local, mesh=mesh, in_specs=in_specs, out_specs=out_specs, check_vma=False)
```

profile of v0, /device:TPU:2, one launch (start us, length us, event | category | flops | bytes accessed | tf_op | source)
XLA Modules:
  0.0 463.6 jit_solution(8965409141635587499)
XLA Ops:
  7.2 27.8 %all_gather.12 = f32[1024,64]{1,0:T(8,128)S(1)} all-gather(f32[32,64]{1,0:T(8,128)} %param.8), channel_id=1, replica_groups=mesh['row'=32,'col'=16] {'row'}, dimensions={0}, use_global_device_ids=true | all-gather | bytes 270336 | tf_op jit(solution)/shard_map/all_gather | solution.py:25
  35.0 0.9 copy.14
  36.0 0.7 all-gather.6.cloned.1.call-update
  36.7 0.7 all-gather.8.cloned.1.call-update
  37.5 77.2 %all-gather.4.cloned.1.call-done = f32[1024,1024]{0,1:T(8,128)} async-done(((f32[1024,64]{0,1:T(8,128)}), f32[1024,1024]{0,1:T(8,128)}) %all-gather.4.cloned.1.call-update) | async-done | bytes 4194320 | tf_op jit(solution)/shard_map/all_gather | solution.py:26
  114.7 4.8 %fusion = f32[1024,1024]{0,1:T(8,128)} fusion(f32[1024,1024]{0,1:T(8,128)} %all-gather.4.cloned.1.call-done), kind=kLoop, calls=%fused_computation.3 | loop fusion | flops 2097152 | bytes 8388608 | tf_op jit(solution)/shard_map/jit(_solve_triangular)/triangular_solve | solution.py:8
  119.5 24.1 %while.1 = (s32[]{:T(128)}, f32[1024,1024]{0,1:T(8,128)}, s32[8,2]{0,1:T(2,128)S(1)}, f32[8,128,128]{2,1,0:T(8,128)S(1)}, s32[]{:T(128)}) while((s32[]{:T(128)}, f32[1024,1024]{0,1:T(8,128)}, s32[8,2]{0,1:T(2,128)S(1)}, f32[8,128,128]{2,1,0:T(8,128)S(1)}, s32[]{:T(128)}) %tuple.28), condition=%wide.while_cond, body=%wide.while_body.sunk | while | flops 2 | bytes 393321 | solution.py:8
  119.5 0.5 fusion.55
  120.1 2.3 dynamic-slice.12
  122.6 0.5 fusion.55
  123.1 2.3 dynamic-slice.12
  125.6 0.5 fusion.55
  126.1 2.3 dynamic-slice.12
  128.6 0.5 fusion.55
  129.1 2.3 dynamic-slice.12
  131.6 0.5 fusion.55
  132.2 2.3 dynamic-slice.12
  134.7 0.5 fusion.55
  135.2 2.3 dynamic-slice.12
  137.7 0.5 fusion.55
  138.2 2.3 dynamic-slice.12
  140.7 0.5 fusion.55
  141.2 2.2 dynamic-slice.12
  143.6 78.6 %custom-call.4 = f32[8,128,128]{1,2,0:T(8,128)S(1)} custom-call(f32[8,128,128]{2,1,0:T(8,128)S(1)} %get-tuple-element.11), custom_call_target="InvertDiagBlocksLowerTriangular" | custom-call | tf_op jit(solution)/shard_map/jit(_solve_triangular)/triangular_solve | solution.py:8
  222.2 1.5 fusion.19
  223.8 1.4 convolution_subtract_fusion.4
  225.1 0.4 fusion.25
  225.5 1.4 convolution_subtract_fusion.3
  227.0 0.4 fusion.26
  227.3 1.6 convolution_subtract_fusion.6
  228.9 0.4 fusion.27
  229.3 1.7 convolution_subtract_fusion.7
  230.9 0.4 constant_dynamic-update-slice_fusion.4
  231.4 1.9 convolution_subtract_fusion.2
  233.3 0.4 constant_dynamic-update-slice_fusion.10
  233.8 2.0 convolution_subtract_fusion.5
  235.9 0.4 constant_dynamic-update-slice_fusion.17
  236.4 2.2 convolution_subtract_fusion.1
  238.6 1.2 convolution_dynamic-update-slice_fusion
  240.1 2.6 fusion.36
  242.7 0.3 reduce-scatter.3.cloned.1.call-start
  243.0 4.8 %fusion.35 = f32[1024,512]{1,0:T(8,128)} fusion(f32[1024,512]{1,0:T(8,128)S(1)} %constant_dynamic-update-slice_fusion.18, f32[512,512]{1,0:T(8,128)S(1)} %copy-done), kind=kOutput, calls=%fused_computation.85 | convolution fusion | flops 3221225472 | bytes 5242880 | tf_op jit(solution)/shard_map/rk,rc->kc/dot_general | solution.py:40
  247.8 0.7 dynamic-slice_bitcast_fusion
  248.5 6.3 %convolution_subtract_fusion = f32[512,512]{1,0:T(8,128)} fusion(f32[512,512]{1,0:T(8,128)} %param.13, f32[1024,512]{1,0:T(8,128)S(1)} %constant_dynamic-update-slice_fusion.18, f32[1024,512]{1,0:T(8,128)} %all-gather.8.cloned.1.call-done), kind=kOutput, calls=%fused_computation.4 | convolution fusion | flops 3221487616 | bytes 6291456 | tf_op jit(solution)/shard_map/dot_general | solution.py:31
  254.9 95.1 %reduce-scatter.5.cloned.1.call-done = f32[32,64]{1,0:T(8,128)} async-done(((f32[1024,64]{1,0:T(8,128)}), f32[32,64]{1,0:T(8,128)}) %reduce-scatter.5.cloned.1.call-update) | async-done | bytes 8208 | tf_op jit(solution)/shard_map/reduce_scatter | solution.py:46
  349.9 1.4 select_subtract_fusion
  351.3 104.3 %reduce-scatter.3.cloned.1.call-done = f32[32,512]{1,0:T(8,128)} async-done(((f32[1024,512]{1,0:T(8,128)}), f32[32,512]{1,0:T(8,128)}) %reduce-scatter.3.cloned.1.call-update) | async-done | bytes 65552 | tf_op jit(solution)/shard_map/reduce_scatter | solution.py:39
  455.6 1.5 sub.10
  (72 shorter events, 2.1 us)
Async XLA Ops:
  7.2 235.8 %copy-start = (f32[512,512]{1,0:T(8,128)S(1)}, f32[512,512]{1,0:T(8,128)}, u32[]{:S(2)}) copy-start(f32[512,512]{1,0:T(8,128)} %param.10) | copy-start | bytes 3145732
  7.2 107.5 %all-gather.4.cloned.1.call-start = ((), (), s32[]{:S(2)}) async-start(), calls=%async_computation.2 | async-start | bytes 4456448 | tf_op jit(solution)/shard_map/all_gather | solution.py:26
  35.9 186.3 %all-gather.6.cloned.1.call-start = ((), (), s32[]{:S(2)}) async-start(), calls=%async_computation.3 | async-start | bytes 2228224 | tf_op jit(solution)/shard_map/all_gather | solution.py:27
  36.7 211.8 %all-gather.8.cloned.1.call-start = ((), (), s32[]{:S(2)}) async-start(), calls=%async_computation.4 | async-start | bytes 2162688 | tf_op jit(solution)/shard_map/all_gather | solution.py:33
  37.4 312.5 %reduce-scatter.5.cloned.1.call-start = ((), (), s32[]{:S(2)}) async-start(), calls=%async_computation.6 | async-start | bytes 540672 | tf_op jit(solution)/shard_map/reduce_scatter | solution.py:46
  222.2 13.7 %copy-start.2 = (f32[8,128,128]{1,2,0:T(8,128)}, f32[8,128,128]{1,2,0:T(8,128)S(1)}, u32[]{:S(2)}) copy-start(f32[8,128,128]{1,2,0:T(8,128)S(1)} %custom-call.4) | copy-start | bytes 1572868
  222.2 5.1 %copy-start.1 = (f32[512,1024]{0,1:T(8,128)S(1)}, f32[512,1024]{0,1:T(8,128)}, u32[]{:S(2)}) copy-start(f32[512,1024]{0,1:T(8,128)} %all-gather.6.cloned.1.call-done) | copy-start | bytes 6291460
  238.6 1.5 copy-start.3
  242.7 212.9 %reduce-scatter.3.cloned.1.call-start = ((), (), s32[]{:S(2)}) async-start(), calls=%async_computation.5 | async-start | bytes 2162688 | tf_op jit(solution)/shard_map/reduce_scatter | solution.py:39
  248.5 101.4 %copy-start.5 = (f32[32,64]{1,0:T(8,128)S(1)}, f32[32,64]{1,0:T(8,128)}, u32[]{:S(2)}) copy-start(f32[32,64]{1,0:T(8,128)} %param.15) | copy-start | bytes 24580
  248.5 207.1 %copy-start.4 = (f32[32,512]{1,0:T(8,128)S(1)}, f32[32,512]{1,0:T(8,128)}, u32[]{:S(2)}) copy-start(f32[32,512]{1,0:T(8,128)} %param.14) | copy-start | bytes 196612
Sparse Core Ops, SparseCore 0:
  36.0 78.6 all-gather.3
  116.8 70.5 all-gather.5
  190.5 55.6 all-gather.7
  250.3 99.5 reduce-scatter.4
  354.2 101.3 reduce-scatter.2
where the time goes:
time: 465 us; the launch traced here: 464 us
  waiting for transfers between devices  278 us (60%)
  other arithmetic  86.2 us (19%)
  matrix products  30.8 us (7%)
  blocking collectives  27.8 us (6%)
  local copies, waits for them, and re-layouts  25.9 us (6%)
  between operations  14.2 us (3%)
    reduce_scatter x1, waiting for transfers between devices, local(): lax.psum_scatter(jnp.einsum('rk,rc->kc', picked, left_factor, precision=h...  104 us
    reduce_scatter x1, waiting for transfers between devices, local(): lax.psum_scatter(jnp.einsum('rk,rc->kc', picked, panel_factor, precision=...  95.1 us
    another operation x3, other arithmetic, right_solve(): jax.scipy.linalg.solve_triangular(tile, source.T, trans='T', lower=True)  83.4 us
    all_gather x1, waiting for transfers between devices, local(): whole_diag = lax.all_gather(column_block, 'col', axis=1, tiled=True)  77.2 us
    all_gather x1, blocking collectives, local(): column_block = lax.all_gather(diag_factor, 'row', axis=0, tiled=True)  27.8 us
    another operation x40, local copies, waits for them, and re-layouts  23.8 us
    another operation x15, matrix products, right_solve(): jax.scipy.linalg.solve_triangular(tile, source.T, trans='T', lower=True)  17.1 us
  transfers between devices with their start and end apart: 5, of which 3 were waited for; matrix products, arithmetic and copies ran while one was open for 30% of the time, Pallas kernels for 0%

commit v1 on v0

--- a/solution.py
+++ b/solution.py
@@ -18,11 +18,18 @@
     pivot_adjoint,
     diag_adjoint,
 ):
+
+    def extend_matrix(net_axis, message):
+        lower = jnp.concatenate(
+            tuple((message for _ in range(lax.psum(1, axis_name=net_axis)))), axis=0
+        )
+        return lax.all_to_all(lower, net_axis, 0, 0, tiled=True)
+
     highest = lax.Precision.HIGHEST
     block_width = panel_adjoint.shape[1]
     my_col = lax.axis_index("col")
     my_row = lax.axis_index("row")
-    column_block = lax.all_gather(diag_factor, "row", axis=0, tiled=True)
+    column_block = extend_matrix("row", diag_factor)
     whole_diag = lax.all_gather(column_block, "col", axis=1, tiled=True)
     full_rows = lax.all_gather(panel_adjoint, "col", axis=1, tiled=True)
     solved = right_solve(whole_diag, full_rows)

time: 465 us -> 481 us (1.034)
  local copies, waits for them, and re-layouts: 25.9 us -> 50 us
  blocking collectives: 27.8 us -> 16.4 us
    all_gather x1 -> x0, blocking collectives: 27.8 us -> none  [local(): column_block = lax.all_gather(diag_factor, 'row', axis=0, tiled=True)]
    unnamed x30 -> x63, local copies, waits for them, and re-layouts: 0.39 us -> 23.3 us
    all_to_all x0 -> x1, blocking collectives: none -> 16.4 us  [extend_matrix(): return lax.all_to_all(lower, net_axis, 0, 0, tiled=True)]
  transfers between devices with their start and end apart: 5 -> 5, of which waited for: 3 -> 3; matrix products, arithmetic and copies ran while one was open for 30% -> 29% of each run, Pallas kernels for 0% -> 0%
where the time goes in v1:
time: 481 us; the launch traced here: 478 us
  waiting for transfers between devices  279 us (58%)
  other arithmetic  87.5 us (18%)
  local copies, waits for them, and re-layouts  50 us (10%)
  matrix products  30.8 us (6%)
  blocking collectives  16.4 us (3%)
  between operations  14.2 us (3%)
    reduce_scatter x1, waiting for transfers between devices, local(): lax.psum_scatter(jnp.einsum('rk,rc->kc', picked, left_factor, precision=h...  104 us
    reduce_scatter x1, waiting for transfers between devices, local(): lax.psum_scatter(jnp.einsum('rk,rc->kc', picked, panel_factor, precision=...  95.3 us
    another operation x3, other arithmetic, right_solve(): jax.scipy.linalg.solve_triangular(tile, source.T, trans='T', lower=True)  83.4 us
    all_gather x1, waiting for transfers between devices, local(): whole_diag = lax.all_gather(column_block, 'col', axis=1, tiled=True)  77.9 us
    another operation x40, local copies, waits for them, and re-layouts  23.8 us
    unnamed x63, local copies, waits for them, and re-layouts  23.3 us
    another operation x15, matrix products, right_solve(): jax.scipy.linalg.solve_triangular(tile, source.T, trans='T', lower=True)  17.1 us
    all_to_all x1, blocking collectives, extend_matrix(): return lax.all_to_all(lower, net_axis, 0, 0, tiled=True)  16.4 us
  transfers between devices with their start and end apart: 5, of which 3 were waited for; matrix products, arithmetic and copies ran while one was open for 29% of the time, Pallas kernels for 0%

profile of v1, /device:TPU:2, one launch (start us, length us, event | category | flops | bytes accessed | tf_op | source)
XLA Modules:
  0.0 478.5 jit_solution(5396131247782912949)
XLA Ops:
  7.2 0.8 constant_dynamic-update-slice_fusion.31
  8.0 0.7 constant_dynamic-update-slice_fusion.30
  8.7 0.7 constant_dynamic-update-slice_fusion.29
  9.5 0.7 constant_dynamic-update-slice_fusion.28
  10.2 0.7 constant_dynamic-update-slice_fusion.27
  10.9 0.7 constant_dynamic-update-slice_fusion.26
  11.6 0.7 constant_dynamic-update-slice_fusion.25
  12.3 0.7 constant_dynamic-update-slice_fusion.24
  13.1 0.7 constant_dynamic-update-slice_fusion.23
  13.8 0.7 constant_dynamic-update-slice_fusion.22
  14.5 0.7 constant_dynamic-update-slice_fusion.21
  15.2 0.7 constant_dynamic-update-slice_fusion.20
  15.9 0.7 constant_dynamic-update-slice_fusion.19
  16.7 0.7 constant_dynamic-update-slice_fusion.18
  17.4 0.7 constant_dynamic-update-slice_fusion.17
  18.1 0.7 constant_dynamic-update-slice_fusion.16
  28.9 0.7 constant_dynamic-update-slice_fusion.1
  30.6 16.4 %all_to_all.12 = f32[32,1,2048]{2,1,0:T(1,128)S(1)} all-to-all(f32[32,1,2048]{2,1,0:T(1,128)S(1)} %reshape.53), channel_id=1, replica_groups=mesh['row'=32,'col'=16] {'row'}, dimensions={0} | all-to-all | bytes 524288 | tf_op jit(solution)/shard_map/all_to_all | solution.py:26
  47.5 1.3 reduce
  49.0 0.9 copy.14
  51.5 77.9 %all-gather.4.cloned.1.call-done = f32[1024,1024]{0,1:T(8,128)} async-done(((f32[1024,64]{0,1:T(8,128)}), f32[1024,1024]{0,1:T(8,128)}) %all-gather.4.cloned.1.call-update) | async-done | bytes 4194320 | tf_op jit(solution)/shard_map/all_gather | solution.py:33
  129.4 4.8 fusion
  134.2 24.1 %while.1 = (s32[]{:T(128)}, f32[1024,1024]{0,1:T(8,128)}, s32[8,2]{0,1:T(2,128)S(1)}, f32[8,128,128]{2,1,0:T(8,128)S(1)}, s32[]{:T(128)}) while((s32[]{:T(128)}, f32[1024,1024]{0,1:T(8,128)}, s32[8,2]{0,1:T(2,128)S(1)}, f32[8,128,128]{2,1,0:T(8,128)S(1)}, s32[]{:T(128)}) %tuple.28), condition=%wide.while_cond, body=%wide.while_body.sunk | while | flops 2 | bytes 393321 | solution.py:8
  134.8 2.3 dynamic-slice.12
  137.8 2.3 dynamic-slice.12
  140.8 2.3 dynamic-slice.12
  143.8 2.3 dynamic-slice.12
  146.9 2.3 dynamic-slice.12
  149.9 2.3 dynamic-slice.12
  152.9 2.3 dynamic-slice.12
  155.9 2.2 dynamic-slice.12
  158.3 78.6 %custom-call.4 = f32[8,128,128]{1,2,0:T(8,128)S(1)} custom-call(f32[8,128,128]{2,1,0:T(8,128)S(1)} %get-tuple-element.11), custom_call_target="InvertDiagBlocksLowerTriangular" | custom-call | tf_op jit(solution)/shard_map/jit(_solve_triangular)/triangular_solve | solution.py:8
  236.9 1.5 fusion.19
  238.5 1.4 convolution_subtract_fusion.4
  240.2 1.4 convolution_subtract_fusion.3
  242.0 1.6 convolution_subtract_fusion.6
  244.0 1.7 convolution_subtract_fusion.7
  246.1 1.9 convolution_subtract_fusion.2
  248.5 2.0 convolution_subtract_fusion.5
  251.1 2.2 convolution_subtract_fusion.1
  253.4 1.2 convolution_dynamic-update-slice_fusion
  254.8 2.6 fusion.36
  257.7 4.8 %fusion.35 = f32[1024,512]{1,0:T(8,128)} fusion(f32[1024,512]{1,0:T(8,128)S(1)} %constant_dynamic-update-slice_fusion.50, f32[512,512]{1,0:T(8,128)S(1)} %copy-done), kind=kOutput, calls=%fused_computation.117 | convolution fusion | flops 3221225472 | bytes 5242880 | tf_op jit(solution)/shard_map/rk,rc->kc/dot_general | solution.py:47
  263.2 6.4 %convolution_subtract_fusion = f32[512,512]{1,0:T(8,128)} fusion(f32[512,512]{1,0:T(8,128)} %param.13, f32[1024,512]{1,0:T(8,128)S(1)} %constant_dynamic-update-slice_fusion.50, f32[1024,512]{1,0:T(8,128)} %all-gather.8.cloned.1.call-done), kind=kOutput, calls=%fused_computation.4 | convolution fusion | flops 3221487616 | bytes 6291456 | tf_op jit(solution)/shard_map/dot_general | solution.py:38
  269.6 95.3 %reduce-scatter.5.cloned.1.call-done = f32[32,64]{1,0:T(8,128)} async-done(((f32[1024,64]{1,0:T(8,128)}), f32[32,64]{1,0:T(8,128)}) %reduce-scatter.5.cloned.1.call-update) | async-done | bytes 8208 | tf_op jit(solution)/shard_map/reduce_scatter | solution.py:53
  364.9 1.4 select_subtract_fusion
  366.3 104.2 %reduce-scatter.3.cloned.1.call-done = f32[32,512]{1,0:T(8,128)} async-done(((f32[1024,512]{1,0:T(8,128)}), f32[32,512]{1,0:T(8,128)}) %reduce-scatter.3.cloned.1.call-update) | async-done | bytes 65552 | tf_op jit(solution)/shard_map/reduce_scatter | solution.py:46
  470.5 1.5 sub.10
  (108 shorter events, 22.6 us)
Async XLA Ops:
  7.2 250.5 %copy-start = (f32[512,512]{1,0:T(8,128)S(1)}, f32[512,512]{1,0:T(8,128)}, u32[]{:S(2)}) copy-start(f32[512,512]{1,0:T(8,128)} %param.10) | copy-start | bytes 3145732
  7.2 122.2 %all-gather.4.cloned.1.call-start = ((), (), s32[]{:S(2)}) async-start(), calls=%async_computation.3 | async-start | bytes 4456448 | tf_op jit(solution)/shard_map/all_gather | solution.py:33
  49.9 187.0 %all-gather.6.cloned.1.call-start = ((), (), s32[]{:S(2)}) async-start(), calls=%async_computation.4 | async-start | bytes 2228224 | tf_op jit(solution)/shard_map/all_gather | solution.py:34
  50.7 212.5 %all-gather.8.cloned.1.call-start = ((), (), s32[]{:S(2)}) async-start(), calls=%async_computation.5 | async-start | bytes 2162688 | tf_op jit(solution)/shard_map/all_gather | solution.py:40
  51.4 313.5 %reduce-scatter.5.cloned.1.call-start = ((), (), s32[]{:S(2)}) async-start(), calls=%async_computation.7 | async-start | bytes 540672 | tf_op jit(solution)/shard_map/reduce_scatter | solution.py:53
  236.9 13.7 %copy-start.2 = (f32[8,128,128]{1,2,0:T(8,128)}, f32[8,128,128]{1,2,0:T(8,128)S(1)}, u32[]{:S(2)}) copy-start(f32[8,128,128]{1,2,0:T(8,128)S(1)} %custom-call.4) | copy-start | bytes 1572868
  236.9 5.1 %copy-start.1 = (f32[512,1024]{0,1:T(8,128)S(1)}, f32[512,1024]{0,1:T(8,128)}, u32[]{:S(2)}) copy-start(f32[512,1024]{0,1:T(8,128)} %all-gather.6.cloned.1.call-done) | copy-start | bytes 6291460
  253.3 1.5 copy-start.3
  257.4 213.0 %reduce-scatter.3.cloned.1.call-start = ((), (), s32[]{:S(2)}) async-start(), calls=%async_computation.6 | async-start | bytes 2162688 | tf_op jit(solution)/shard_map/reduce_scatter | solution.py:46
  263.2 101.7 %copy-start.5 = (f32[32,64]{1,0:T(8,128)S(1)}, f32[32,64]{1,0:T(8,128)}, u32[]{:S(2)}) copy-start(f32[32,64]{1,0:T(8,128)} %param.15) | copy-start | bytes 24580
  263.2 207.2 %copy-start.4 = (f32[32,512]{1,0:T(8,128)S(1)}, f32[32,512]{1,0:T(8,128)}, u32[]{:S(2)}) copy-start(f32[32,512]{1,0:T(8,128)} %param.14) | copy-start | bytes 196612
Sparse Core Ops, SparseCore 0:
  50.1 79.2 all-gather.3
  131.5 70.2 all-gather.5
  204.9 56.1 all-gather.7
  265.3 99.5 reduce-scatter.4
  369.1 101.2 reduce-scatter.2
